TPU v7x, 32 devices: a whole 2x2x4 slice. The times are simulated.
32 devices in a mesh: px: 4 (over x, core), py: 8 (over z, y).
Axes of the slice: x: 2, y: 2, z: 4, core: 2. Of those that a mesh axis runs over, the one named last changes fastest.
Arguments:
- adjoint: float32 [8, 8, 8, 1024], P('px', 'py'), may hold values from -6 to 6
- zone_ids: int32 [8, 8, 2], P('px', 'py'), may hold values from 0 to 7
- resist: float32 [8, 8, 2], P('px', 'py'), may hold values from 0.3 to 3
- tile_map: int32 [8, 8, 2], P('px', 'py'), may hold values from 0 to 63, as said below
- materials: float32 [3, 8, 14], replicated, may hold values from 0.2 to 1.5
Outputs:
- applied: float32 [3, 8, 8, 8, 1024], P(None, 'px', 'py')
- tile_grad: float32 [3, 64], P(None, ('px', 'py'))
Inputs may be any that keep to these rules, and one draw needn't show every extreme that they name: `tile_map`: each design tile is a patch of 1 by 1 element columns through the whole thickness; in each row of patches the borders along the first direction may be shifted by one element, and a patch that crosses the panel's first-direction edge continues at the far edge. Tile numbers are in no spatial order, and every tile number occurs.
All inputs are finite; a program needn't handle non-finite values.
Results may differ from a plain program's by a relative error of at most 0.0001.
Values sent between devices are 32-bit elements; how exact they have to be, the bound alone decides.
A program may use at most 64 MiB of HBM per device.

v0:
```python
import functools

import jax
import jax.numpy as jnp
import ml_dtypes
import numpy as np
from jax import lax
from jax.experimental import pallas as pl
from jax.experimental.pallas import tpu as pltpu
from jax.sharding import PartitionSpec as P

NP = 8
FREQS = 3
TILE_DEV = 2
CHANNELS = 8
GRAD_SCALE = 0.001
MESH = pl.DeviceIdType.MESH


def legendre_values(points, point_count):
    values = np.zeros((points.shape[0], point_count))
    values[:, 0] = 1.0
    values[:, 1] = points
    for degree in range(2, point_count):
        values[:, degree] = (
            (2 * degree - 1) * points * values[:, degree - 1] - (degree - 1) * values[:, degree - 2]
        ) / degree
    return values


def lobatto(point_count):
    degree_top = point_count - 1
    points = np.cos(np.pi * np.arange(point_count) / degree_top)
    for newton_step in range(40):
        values = legendre_values(points, point_count)
        points = points - (points * values[:, degree_top] - values[:, degree_top - 1]) / (
            point_count * values[:, degree_top]
        )
    points = points[::-1]
    top_values = legendre_values(points, point_count)[:, degree_top]
    weights = 2.0 / (degree_top * point_count * top_values**2)
    differ = np.zeros((point_count, point_count))
    for row_index in range(point_count):
        for column_index in range(point_count):
            if row_index != column_index:
                differ[row_index, column_index] = top_values[row_index] / (
                    top_values[column_index] * (points[row_index] - points[column_index])
                )
    differ[0, 0] = -degree_top * point_count / 4.0
    differ[degree_top, degree_top] = degree_top * point_count / 4.0
    return (weights, differ)


def split_np(matrix):
    matrix = matrix.astype(np.float32)
    hi = matrix.astype(ml_dtypes.bfloat16)
    lo = (matrix - hi.astype(np.float32)).astype(ml_dtypes.bfloat16)
    return hi, lo


def tables():
    weights, differ = lobatto(NP)
    order = np.array([0, 2, 4, 6, 1, 3, 5, 7])
    weight = weights[order][:, None] * np.tile(np.kron(weights, weights), 2)[None, :]
    along_i = np.kron(np.eye(16), differ)
    along_j = np.kron(np.eye(2), np.kron(differ, np.eye(8)))
    along_k = np.kron(np.eye(16), differ[order][:, order])
    fwd_hi, fwd_lo = split_np(np.concatenate([along_i.T, along_j.T], axis=1))
    back_hi, back_lo = split_np(np.concatenate([along_i, along_j], axis=0))
    k_hi, k_lo = split_np(along_k)
    kt_hi, kt_lo = split_np(along_k.T)
    return (
        np.concatenate([fwd_hi, fwd_lo, fwd_hi], axis=0),
        np.concatenate([k_hi, k_hi, k_lo], axis=1),
        np.concatenate([back_hi, back_lo, back_hi], axis=0),
        np.concatenate([kt_hi, kt_hi, kt_lo], axis=1),
        np.tile(weight, (2, 1)).astype(np.float32),
    )


def split(values):
    hi = values.astype(jnp.bfloat16)
    lo = (values - hi.astype(jnp.float32)).astype(jnp.bfloat16)
    return hi, lo


def conj_times(c, x):
    return (c[0] * x[0] + c[1] * x[1], c[0] * x[1] - c[1] * x[0])


def plus(left, right):
    return (left[0] + right[0], left[1] + right[1])


def minus(left, right):
    return (left[0] - right[0], left[1] - right[1])


def body(
    npx,
    npy,
    x_ref,
    zone_ref,
    resist_ref,
    tile_ref,
    mat_ref,
    fwd_ref,
    fwdk_ref,
    back_ref,
    backk_ref,
    weight_ref,
    out_ref,
    grad_ref,
    held,
    sxb,
    syb,
    rx,
    ry,
    rc,
    g1,
    g2,
    x_send,
    x_recv,
    y_send,
    y_recv,
    c_send,
    c_recv,
    g1_send,
    g1_recv,
    g2_send,
    g2_recv,
):
    f32 = jnp.float32
    px, py = lax.axis_index("px"), lax.axis_index("py")
    to_x = (px - 1, px + 1)
    to_y = (py - 1, py + 1)
    has_x = (px > 0, px < npx - 1)
    has_y = (py > 0, py < npy - 1)
    corners = [(i, j) for i in range(2) for j in range(2)]

    def has_corner(i, j):
        return jnp.logical_and(has_x[i], has_y[j])

    def peer_px(d):
        return (lax.rem(px + d, npx), py)

    def peer_py(d):
        return (px, lax.rem(py + d, npy))

    def over(count, step):
        if count <= 8:
            for d in range(1, count):
                step(d)
        else:
            lax.fori_loop(1, count, lambda d, carry: (step(d), carry)[1], 0)

    barrier = pltpu.get_barrier_semaphore()

    def greet(device):
        pl.semaphore_signal(barrier, inc=1, device_id=device, device_id_type=MESH)

    over(npx, lambda d: greet(peer_px(d)))
    over(npy, lambda d: greet(peer_py(d)))
    for i, j in corners:

        @pl.when(has_corner(i, j))
        def _(i=i, j=j):
            greet((to_x[i], to_y[j]))

    x_sides = jnp.where(has_x[0], 1, 0) + jnp.where(has_x[1], 1, 0)
    y_sides = jnp.where(has_y[0], 1, 0) + jnp.where(has_y[1], 1, 0)

    row = lax.broadcasted_iota(jnp.int32, (8, 128), 0)
    lane = lax.broadcasted_iota(jnp.int32, (8, 128), 1)
    low = lane < 64
    keep = (row < 4) == low
    at_i = (lane % 8 == 0, lane % 8 == 7)
    at_j = ((lane // 8) % 8 == 0, (lane // 8) % 8 == 7)
    slot_i = [lane % 8 == m for m in range(8)]
    slot_j = [(lane // 8) % 8 == m for m in range(8)]
    seam_low = jnp.logical_and(row == 3, lane >= 64)
    seam_high = jnp.logical_and(row == 4, low)

    def lane_roll(block, shift):
        shift = shift % 128
        return block if shift == 0 else pltpu.roll(block, shift, 1)

    def swap(block):
        return jnp.where(keep, block, pltpu.roll(lane_roll(block, 64), 4, 0))

    for i in range(2):

        @pl.when(jnp.logical_not(has_x[i]))
        def _(i=i):
            rx[i] = jnp.zeros((FREQS, 8, 128), f32)

        @pl.when(jnp.logical_not(has_y[i]))
        def _(i=i):
            ry[i] = jnp.zeros((2, FREQS, 8, 128), f32)

    for i, j in corners:

        @pl.when(jnp.logical_not(has_corner(i, j)))
        def _(i=i, j=j):
            rc[2 * i + j] = jnp.zeros((FREQS, 8, 128), f32)

    blocks = []
    for m in range(CHANNELS):
        for a in range(2):
            blocks.append(swap(x_ref[pl.ds(64 * a + m, 8, stride=8), :]))
    nodal = jnp.concatenate(blocks, axis=0)
    hi, lo = split(nodal)
    first_two = jnp.dot(
        jnp.concatenate([hi, hi, lo], axis=1), fwd_ref[...], preferred_element_type=f32
    )
    third = jnp.dot(
        fwdk_ref[...], jnp.concatenate([hi, lo, hi], axis=0), preferred_element_type=f32
    )
    raw = (first_two[:, :128], first_two[:, 128:], third)
    weight = weight_ref[...]

    def channel(source, m):
        return source[16 * m : 16 * m + 16]

    def pair(source, m):
        return (weight * channel(source, m), weight * channel(source, m + 4))

    u = [pair(nodal, m) for m in range(4)]
    g = [[pair(raw[d], m) for m in range(4)] for d in range(3)]

    zones = [[zone_ref[a, 0, c] for c in range(2)] for a in range(2)]

    def spread(get):
        return jnp.concatenate(
            [jnp.where(low, get(a, 0), get(a, 1)) for a in range(2)], axis=0
        )

    resist = spread(lambda a, c: resist_ref[a, 0, c])
    coeffs = []
    slopes = []
    for f in range(FREQS):
        col = [spread(lambda a, c: mat_ref[f, zones[a][c], n]) for n in range(14)]
        density, gain = col[10], col[11]
        damping = resist * gain
        inverse = 1.0 / (density * density + damping * damping)
        real, imag = density * inverse, damping * inverse
        mobility = (col[8] * real - col[9] * imag, col[8] * imag + col[9] * real)
        square = gain * inverse * inverse
        real = -2.0 * density * damping * square
        imag = (density * density - damping * damping) * square
        slopes.append((col[8] * real - col[9] * imag, col[8] * imag + col[9] * real))
        coeffs.append(
            (
                (col[0], col[1]),
                (col[2], col[3]),
                (col[4], col[5]),
                (col[6], col[7]),
                mobility,
                (col[12], col[13]),
            )
        )

    energy_real = jnp.zeros((16, 128), f32)
    energy_imag = jnp.zeros((16, 128), f32)
    for d in range(3):
        real, imag = channel(raw[d], 3), channel(raw[d], 7)
        energy_real += g[d][3][0] * real - g[d][3][1] * imag
        energy_imag += g[d][3][0] * imag
    energy_imag = 2.0 * energy_imag
    width = g1.shape[2]
    wide = lax.broadcasted_iota(jnp.int32, (8, width), 1)
    wide_row = lax.broadcasted_iota(jnp.int32, (8, width), 0)
    message = jnp.zeros((8, width), f32)
    for f in range(FREQS):
        density = GRAD_SCALE * (slopes[f][0] * energy_real + slopes[f][1] * energy_imag)
        gathered = jnp.zeros((8, width), f32)
        for a in range(2):
            part = density[8 * a : 8 * a + 8]
            for c in range(2):
                mine = jnp.where(low, part, 0.0) if c == 0 else jnp.where(low, 0.0, part)
                mine = jnp.sum(mine, axis=1, keepdims=True)
                gathered += jnp.where(wide == tile_ref[a, 0, c], mine, 0.0)
        gathered = jnp.sum(gathered, axis=0, keepdims=True)
        message = jnp.where(wide_row == f, gathered, message)
    g1[0] = message

    pl.semaphore_wait(barrier, npx - 1 + npy - 1 + x_sides * y_sides)

    def copy_g1(d):
        return pltpu.make_async_remote_copy(
            src_ref=g1.at[0],
            dst_ref=g1.at[d],
            send_sem=g1_send.at[d],
            recv_sem=g1_recv.at[d],
            device_id=peer_px(d),
            device_id_type=MESH,
        )

    def copy_g2(d):
        return pltpu.make_async_remote_copy(
            src_ref=g2.at[0],
            dst_ref=g2.at[d],
            send_sem=g2_send.at[d],
            recv_sem=g2_recv.at[d],
            device_id=peer_py(d),
            device_id_type=MESH,
        )

    over(npx, lambda d: copy_g1(d).start())

    div = plus(plus(g[0][0], g[1][1]), g[2][2])
    sym = {}
    for m in range(3):
        for d in range(m, 3):
            sym[m, d] = plus(g[d][m], g[m][d])

    for f in range(FREQS):
        lame, shear, inertia, coupling, mobility, storage = coeffs[f]
        lame_term = conj_times(lame, div)
        stress = {}
        for (m, d), value in sym.items():
            item = conj_times(shear, value)
            if m == d:
                item = plus(item, lame_term)
            stress[m, d] = stress[d, m] = item
        flux = []
        for d in range(3):
            fluid = minus(conj_times(mobility, g[d][3]), conj_times(coupling, u[d]))
            items = [stress[m, d] for m in range(3)] + [fluid]
            flux.append(
                split(
                    jnp.concatenate([item[0] for item in items] + [item[1] for item in items], axis=0)
                )
            )
        items = [
            plus(conj_times(inertia, u[m]), conj_times(coupling, g[m][3])) for m in range(3)
        ] + [conj_times(storage, u[3])]
        local = jnp.concatenate([item[0] for item in items] + [item[1] for item in items], axis=0)
        (i_hi, i_lo), (j_hi, j_lo), (k_hi, k_lo) = flux
        total = jnp.dot(
            jnp.concatenate([i_hi, j_hi, i_hi, j_hi, i_lo, j_lo], axis=1),
            back_ref[...],
            preferred_element_type=f32,
        )
        total += jnp.dot(
            backk_ref[...], jnp.concatenate([k_hi, k_lo, k_hi], axis=0), preferred_element_type=f32
        )
        total -= local
        packed_x = [jnp.zeros((8, 128), f32)] * 2
        packed_y = [[jnp.zeros((8, 128), f32)] * 2 for _ in range(2)]
        for m in range(CHANNELS):
            both = []
            for a in range(2):
                block = swap(total[16 * m + 8 * a : 16 * m + 8 * a + 8])
                turned = lane_roll(block, 64)
                block = (
                    block
                    + jnp.where(seam_low, pltpu.roll(turned, 7, 0), 0.0)
                    + jnp.where(seam_high, pltpu.roll(turned, 1, 0), 0.0)
                )
                both.append(block)
            left, right = both
            both = [
                left + jnp.where(at_i[1], lane_roll(right, 7), 0.0),
                right + jnp.where(at_i[0], lane_roll(left, -7), 0.0),
            ]
            for s in range(2):
                packed_x[s] = jnp.where(slot_i[m], lane_roll(both[s], m - 7 * s), packed_x[s])
                for a in range(2):
                    packed_y[s][a] = jnp.where(
                        slot_j[m], lane_roll(both[a], 8 * (m - 7 * s)), packed_y[s][a]
                    )
            for a in range(2):
                held[f, 2 * m + a] = both[a]
        for s in range(2):
            sxb[s, f] = packed_x[s]
            for a in range(2):
                syb[s, a, f] = packed_y[s][a]

    def copy_x(s, there):
        return pltpu.make_async_remote_copy(
            src_ref=sxb.at[s],
            dst_ref=rx.at[there],
            send_sem=x_send.at[s],
            recv_sem=x_recv.at[there],
            device_id=(to_x[s], py),
            device_id_type=MESH,
        )

    def copy_y(s, there):
        return pltpu.make_async_remote_copy(
            src_ref=syb.at[s],
            dst_ref=ry.at[there],
            send_sem=y_send.at[s],
            recv_sem=y_recv.at[there],
            device_id=(px, to_y[s]),
            device_id_type=MESH,
        )

    def copy_c(i, j, there):
        return pltpu.make_async_remote_copy(
            src_ref=syb.at[j, i],
            dst_ref=rc.at[there],
            send_sem=c_send.at[2 * i + j],
            recv_sem=c_recv.at[there],
            device_id=(to_x[i], to_y[j]),
            device_id_type=MESH,
        )

    for s in range(2):

        @pl.when(has_y[s])
        def _(s=s):
            copy_y(s, 1 - s).start()

    for i, j in corners:

        @pl.when(has_corner(i, j))
        def _(i=i, j=j):
            copy_c(i, j, 3 - 2 * i - j).start()

    for s in range(2):

        @pl.when(has_x[s])
        def _(s=s):
            copy_x(s, 1 - s).start()

    over(npx, lambda d: copy_g1(d).wait())
    column = g1[0]
    for d in range(1, npx):
        column += g1[d]
    g2[0] = column
    over(npy, lambda d: copy_g2(d).start())

    for s in range(2):

        @pl.when(has_x[s])
        def _(s=s):
            copy_x(s, s).wait()

    for s in range(2):

        @pl.when(has_y[s])
        def _(s=s):
            copy_y(s, s).wait()

    for i, j in corners:

        @pl.when(has_corner(i, j))
        def _(i=i, j=j):
            copy_c(i, j, 2 * i + j).wait()

    for f in range(FREQS):
        from_x = [rx[s, f] for s in range(2)]
        from_y = []
        for s in range(2):
            side = []
            for a in range(2):
                corner = lane_roll(rc[2 * a + s, f], 7 * (2 * a - 1))
                side.append(ry[s, a, f] + jnp.where(at_i[a], corner, 0.0))
            from_y.append(side)
        for m in range(CHANNELS):
            for a in range(2):
                block = held[f, 2 * m + a]
                block += jnp.where(at_i[a], lane_roll(from_x[a], 7 * a - m), 0.0)
                for s in range(2):
                    block += jnp.where(
                        at_j[s], lane_roll(from_y[s][a], 8 * (7 * s - m)), 0.0
                    )
                out_ref[pl.ds(128 * f + 64 * a + m, 8, stride=8), :] = block

    over(npy, lambda d: copy_g2(d).wait())
    if npy <= 8:
        column = g2[0]
        for d in range(1, npy):
            column += g2[d]
    else:
        column = lax.fori_loop(1, npy, lambda d, carry: carry + g2[d], g2[0])
    first = TILE_DEV * (px * npy + py)
    pieces = [
        jnp.sum(jnp.where(wide == first + q, column, 0.0), axis=1, keepdims=True)
        for q in range(TILE_DEV)
    ]
    grad_ref[...] = jnp.concatenate(pieces, axis=1)[:FREQS]


def on_device(npx, npy, adjoint, zone_ids, resist, tile_map, materials):
    f32 = jnp.float32
    view = adjoint.reshape(2, 8, 8, 128).transpose(0, 2, 1, 3).reshape(128, 128)
    width = -(-TILE_DEV * npx * npy // 128) * 128
    vmem = pl.BlockSpec(memory_space=pltpu.VMEM)
    smem = pl.BlockSpec(memory_space=pltpu.SMEM)
    dma = pltpu.SemaphoreType.DMA
    out, grad = pl.pallas_call(
        functools.partial(body, npx, npy),
        out_shape=(
            jax.ShapeDtypeStruct((FREQS * 128, 128), f32),
            jax.ShapeDtypeStruct((FREQS, TILE_DEV), f32),
        ),
        in_specs=[vmem] + [smem] * 4 + [vmem] * 5,
        out_specs=(vmem, vmem),
        scratch_shapes=[
            pltpu.VMEM((FREQS, 16, 8, 128), f32),
            pltpu.VMEM((2, FREQS, 8, 128), f32),
            pltpu.VMEM((2, 2, FREQS, 8, 128), f32),
            pltpu.VMEM((2, FREQS, 8, 128), f32),
            pltpu.VMEM((2, 2, FREQS, 8, 128), f32),
            pltpu.VMEM((4, FREQS, 8, 128), f32),
            pltpu.VMEM((npx, 8, width), f32),
            pltpu.VMEM((npy, 8, width), f32),
            dma((2,)),
            dma((2,)),
            dma((2,)),
            dma((2,)),
            dma((4,)),
            dma((4,)),
            dma((npx,)),
            dma((npx,)),
            dma((npy,)),
            dma((npy,)),
        ],
        compiler_params=pltpu.CompilerParams(
            collective_id=0, has_side_effects=True, vmem_limit_bytes=32 * 1024 * 1024
        ),
    )(view, zone_ids, resist, tile_map, materials, *[jnp.asarray(item) for item in tables()])
    applied = out.reshape(FREQS, 2, 8, 8, 128).transpose(0, 1, 3, 2, 4)
    return (applied.reshape(FREQS, 2, 1, CHANNELS, 1024), grad)


def solution(mesh):
    in_specs = (
        P("px", "py", None, None),
        P("px", "py", None),
        P("px", "py", None),
        P("px", "py", None),
        P(),
    )
    out_specs = (P(None, "px", "py", None, None), P(None, ("px", "py")))
    return jax.shard_map(
        functools.partial(on_device, mesh.shape["px"], mesh.shape["py"]),
        mesh=mesh,
        in_specs=in_specs,
        out_specs=out_specs,
        check_vma=False,
    )
```

profile of v0, /device:TPU:0, one launch (start us, length us, event | category | flops | bytes accessed | tf_op | source)
XLA Modules:
  0.0 22.0 jit_solution(18318321669683003652)
XLA Ops:
  0.6 0.0 copy-start.6
  0.6 0.0 copy-start.7
  0.7 0.7 %copy-done.6 = f32[16,128]{1,0:T(8,128)S(1)} copy-done((f32[16,128]{1,0:T(8,128)S(1)}, f32[16,128]{1,0:T(8,128)}, u32[]{:S(2)}) %copy-start.6) | copy-done | bytes 8216
  1.3 0.0 copy-done.7
  1.3 0.0 copy-start
  1.3 0.9 %copy-done = bf16[768,128]{1,0:T(8,128)(2,1)S(1)} copy-done((bf16[768,128]{1,0:T(8,128)(2,1)S(1)}, bf16[768,128]{1,0:T(8,128)(2,1)}, u32[]{:S(2)}) %copy-start) | copy-done | bytes 196632
  2.3 0.0 copy-start.1
  2.3 0.9 %copy-done.1 = bf16[384,256]{1,0:T(8,128)(2,1)S(1)} copy-done((bf16[384,256]{1,0:T(8,128)(2,1)S(1)}, bf16[384,256]{1,0:T(8,128)(2,1)}, u32[]{:S(2)}) %copy-start.1) | copy-done | bytes 196632
  3.2 0.0 copy-start.2
  3.2 0.9 %copy-done.2 = bf16[128,384]{1,0:T(8,128)(2,1)S(1)} copy-done((bf16[128,384]{1,0:T(8,128)(2,1)S(1)}, bf16[128,384]{1,0:T(8,128)(2,1)}, u32[]{:S(2)}) %copy-start.2) | copy-done | bytes 98328
  4.1 0.0 copy-start.3
  4.1 0.9 %copy-done.3 = bf16[128,384]{1,0:T(8,128)(2,1)S(1)} copy-done((bf16[128,384]{1,0:T(8,128)(2,1)S(1)}, bf16[128,384]{1,0:T(8,128)(2,1)}, u32[]{:S(2)}) %copy-start.3) | copy-done | bytes 98328
  5.0 0.0 copy-start.4
  5.0 0.8 %copy-done.4 = f32[2,1,8,1024]{3,2,1,0:T(8,128)S(1)} copy-done((f32[2,1,8,1024]{3,2,1,0:T(8,128)S(1)}, f32[2,1,8,1024]{3,2,1,0:T(8,128)}, u32[]{:S(2)}) %copy-start.4) | copy-done | bytes 65560
  5.8 0.0 copy-start.5
  5.8 0.7 %copy-done.5 = f32[3,8,14]{2,1,0:T(8,128)S(1)} copy-done((f32[3,8,14]{2,1,0:T(8,128)S(1)}, f32[3,8,14]{2,1,0:T(8,128)}, u32[]{:S(2)}) %copy-start.5) | copy-done | bytes 1368
  6.5 0.0 copy-start.8
  6.5 0.7 %copy-done.8 = f32[2,1,2]{2,1,0:T(1,128)S(1)} copy-done((f32[2,1,2]{2,1,0:T(1,128)S(1)}, f32[2,1,2]{2,1,0:T(1,128)}, u32[]{:S(2)}) %copy-start.8) | copy-done | bytes 40
  7.2 0.0 copy-start.9
  7.2 0.7 %copy-done.9 = s32[2,1,2]{2,1,0:T(1,128)S(1)} copy-done((s32[2,1,2]{2,1,0:T(1,128)S(1)}, s32[2,1,2]{2,1,0:T(1,128)}, u32[]{:S(2)}) %copy-start.9) | copy-done | bytes 40
  7.9 12.7 %shard_map.113 = (f32[384,128]{1,0:T(8,128)S(1)}, f32[3,2]{1,0:T(4,128)S(1)}) custom-call(f32[128,128]{1,0:T(8,128)S(1)} %bitcast.11, s32[2,1,2]{2,1,0:T(1,128)S(1)} %copy-done.7, f32[2,1,2]{2,1,0:T(1,128)S(1)} %copy-done.8, s32[2,1,2]{2,1,0:T(1,128)S(1)} %copy-done.9, f32[3,8,14]{2,1,0:T(8,128)S(1)} %copy-done.5, bf16[384,256]{1,0:T(8,128)(2,1)S(1)} %copy-done.1, ...), custom_call_target="tpu_custom_call" | custom-call | tf_op jit(solution)/shard_map/pallas_call | solution.py:494
  20.6 0.6 %copy.12 = f32[3,2]{0,1:T(2,128)} copy(f32[3,2]{1,0:T(4,128)S(1)} %get-tuple-element.7) | data formatting | bytes 48
  21.3 0.7 %copy.14 = f32[3,2,1,8,1024]{4,3,2,1,0:T(8,128)} copy(f32[3,2,1,8,1024]{4,3,2,1,0:T(8,128)S(1)} %bitcast.10) | data formatting | bytes 393216
Async XLA Ops:
  0.6 0.7 %copy-start.6 = (f32[16,128]{1,0:T(8,128)S(1)}, f32[16,128]{1,0:T(8,128)}, u32[]{:S(2)}) copy-start(f32[16,128]{1,0:T(8,128)} %constant.14.clone.weight_ref) | copy-start | bytes 24580
  0.6 0.7 %copy-start.7 = (s32[2,1,2]{2,1,0:T(1,128)S(1)}, s32[2,1,2]{2,1,0:T(1,128)}, u32[]{:S(2)}) copy-start(s32[2,1,2]{2,1,0:T(1,128)} %zone_ref.1) | copy-start | bytes 52
  1.3 0.9 %copy-start = (bf16[768,128]{1,0:T(8,128)(2,1)S(1)}, bf16[768,128]{1,0:T(8,128)(2,1)}, u32[]{:S(2)}) copy-start(bf16[768,128]{1,0:T(8,128)(2,1)} %constant.12.clone.back_ref) | copy-start | bytes 589828
  2.3 0.9 %copy-start.1 = (bf16[384,256]{1,0:T(8,128)(2,1)S(1)}, bf16[384,256]{1,0:T(8,128)(2,1)}, u32[]{:S(2)}) copy-start(bf16[384,256]{1,0:T(8,128)(2,1)} %constant.10.clone.fwd_ref) | copy-start | bytes 589828
  3.2 0.9 %copy-start.2 = (bf16[128,384]{1,0:T(8,128)(2,1)S(1)}, bf16[128,384]{1,0:T(8,128)(2,1)}, u32[]{:S(2)}) copy-start(bf16[128,384]{1,0:T(8,128)(2,1)} %constant.13.clone.backk_ref) | copy-start | bytes 294916
  4.1 0.9 %copy-start.3 = (bf16[128,384]{1,0:T(8,128)(2,1)S(1)}, bf16[128,384]{1,0:T(8,128)(2,1)}, u32[]{:S(2)}) copy-start(bf16[128,384]{1,0:T(8,128)(2,1)} %constant.11.clone.fwdk_ref) | copy-start | bytes 294916
  5.0 0.8 %copy-start.4 = (f32[2,1,8,1024]{3,2,1,0:T(8,128)S(1)}, f32[2,1,8,1024]{3,2,1,0:T(8,128)}, u32[]{:S(2)}) copy-start(f32[2,1,8,1024]{3,2,1,0:T(8,128)} %param.10) | copy-start | bytes 196612
  5.8 0.7 %copy-start.5 = (f32[3,8,14]{2,1,0:T(8,128)S(1)}, f32[3,8,14]{2,1,0:T(8,128)}, u32[]{:S(2)}) copy-start(f32[3,8,14]{2,1,0:T(8,128)} %mat_ref.1) | copy-start | bytes 4036
  6.5 0.7 %copy-start.8 = (f32[2,1,2]{2,1,0:T(1,128)S(1)}, f32[2,1,2]{2,1,0:T(1,128)}, u32[]{:S(2)}) copy-start(f32[2,1,2]{2,1,0:T(1,128)} %resist_ref.1) | copy-start | bytes 52
  7.2 0.7 %copy-start.9 = (s32[2,1,2]{2,1,0:T(1,128)S(1)}, s32[2,1,2]{2,1,0:T(1,128)}, u32[]{:S(2)}) copy-start(s32[2,1,2]{2,1,0:T(1,128)} %tile_ref.1) | copy-start | bytes 52
where the time goes:
time: 22.4 us; the launch traced here: 22 us
  Pallas kernels  12.7 us (57%)
  local copies, waits for them, and re-layouts  8.55 us (38%)
  between operations  0.66 us (3%)
    pallas_call x1, Pallas kernels, on_device(): pl.pallas_call(functools.partial(body, npx, npy), out_shape=(jax.ShapeDty...  12.7 us
    unnamed x22, local copies, waits for them, and re-layouts  8.55 us

commit v1 on v0

--- a/solution.py
+++ b/solution.py
@@ -69,11 +69,10 @@
     back_hi, back_lo = split_np(np.concatenate([along_i, along_j], axis=0))
     k_hi, k_lo = split_np(along_k)
     kt_hi, kt_lo = split_np(along_k.T)
+    forward = np.concatenate([fwd_hi, fwd_lo, fwd_hi], axis=0)
     return (
-        np.concatenate([fwd_hi, fwd_lo, fwd_hi], axis=0),
-        np.concatenate([k_hi, k_hi, k_lo], axis=1),
-        np.concatenate([back_hi, back_lo, back_hi], axis=0),
-        np.concatenate([kt_hi, kt_hi, kt_lo], axis=1),
+        np.concatenate([forward[:, :128], forward[:, 128:], k_hi, k_hi, k_lo], axis=0),
+        np.concatenate([back_hi, back_lo, back_hi, kt_hi, kt_hi, kt_lo], axis=0),
         np.tile(weight, (2, 1)).astype(np.float32),
     )
 
@@ -99,18 +98,25 @@
 def body(
     npx,
     npy,
+    x_hbm,
+    zone_hbm,
+    resist_hbm,
+    tile_hbm,
+    mat_hbm,
+    forward_hbm,
+    backward_hbm,
+    weight_hbm,
+    out_ref,
+    grad_ref,
     x_ref,
     zone_ref,
     resist_ref,
     tile_ref,
     mat_ref,
-    fwd_ref,
-    fwdk_ref,
-    back_ref,
-    backk_ref,
+    forward_ref,
+    backward_ref,
     weight_ref,
-    out_ref,
-    grad_ref,
+    load_sem,
     held,
     sxb,
     syb,
@@ -131,6 +137,23 @@
     g2_recv,
 ):
     f32 = jnp.float32
+    loads = [
+        pltpu.make_async_copy(source, target, load_sem.at[n])
+        for n, (source, target) in enumerate(
+            (
+                (x_hbm, x_ref),
+                (forward_hbm, forward_ref),
+                (weight_hbm, weight_ref),
+                (zone_hbm, zone_ref),
+                (resist_hbm, resist_ref),
+                (mat_hbm, mat_ref),
+                (tile_hbm, tile_ref),
+                (backward_hbm, backward_ref),
+            )
+        )
+    ]
+    for load in loads:
+        load.start()
     px, py = lax.axis_index("px"), lax.axis_index("py")
     to_x = (px - 1, px + 1)
     to_y = (py - 1, py + 1)
@@ -204,19 +227,25 @@
         def _(i=i, j=j):
             rc[2 * i + j] = jnp.zeros((FREQS, 8, 128), f32)
 
+    loads[0].wait()
     blocks = []
     for m in range(CHANNELS):
         for a in range(2):
             blocks.append(swap(x_ref[pl.ds(64 * a + m, 8, stride=8), :]))
     nodal = jnp.concatenate(blocks, axis=0)
     hi, lo = split(nodal)
-    first_two = jnp.dot(
-        jnp.concatenate([hi, hi, lo], axis=1), fwd_ref[...], preferred_element_type=f32
-    )
-    third = jnp.dot(
-        fwdk_ref[...], jnp.concatenate([hi, lo, hi], axis=0), preferred_element_type=f32
-    )
-    raw = (first_two[:, :128], first_two[:, 128:], third)
+    loads[1].wait()
+    wide_nodal = jnp.concatenate([hi, hi, lo], axis=1)
+    first = jnp.dot(wide_nodal, forward_ref[0:384, :], preferred_element_type=f32)
+    second = jnp.dot(wide_nodal, forward_ref[384:768, :], preferred_element_type=f32)
+
+    def left(ref, base, tall):
+        k_parts = [ref[base + 128 * n : base + 128 * n + 128, :] for n in range(3)]
+        return jnp.dot(jnp.concatenate(k_parts, axis=1), tall, preferred_element_type=f32)
+
+    third = left(forward_ref, 768, jnp.concatenate([hi, lo, hi], axis=0))
+    raw = (first, second, third)
+    loads[2].wait()
     weight = weight_ref[...]
 
     def channel(source, m):
@@ -228,6 +257,8 @@
     u = [pair(nodal, m) for m in range(4)]
     g = [[pair(raw[d], m) for m in range(4)] for d in range(3)]
 
+    for load in loads[3:7]:
+        load.wait()
     zones = [[zone_ref[a, 0, c] for c in range(2)] for a in range(2)]
 
     def spread(get):
@@ -314,6 +345,7 @@
         for d in range(m, 3):
             sym[m, d] = plus(g[d][m], g[m][d])
 
+    loads[7].wait()
     for f in range(FREQS):
         lame, shear, inertia, coupling, mobility, storage = coeffs[f]
         lame_term = conj_times(lame, div)
@@ -339,12 +371,10 @@
         (i_hi, i_lo), (j_hi, j_lo), (k_hi, k_lo) = flux
         total = jnp.dot(
             jnp.concatenate([i_hi, j_hi, i_hi, j_hi, i_lo, j_lo], axis=1),
-            back_ref[...],
+            backward_ref[0:768, :],
             preferred_element_type=f32,
         )
-        total += jnp.dot(
-            backk_ref[...], jnp.concatenate([k_hi, k_lo, k_hi], axis=0), preferred_element_type=f32
-        )
+        total += left(backward_ref, 768, jnp.concatenate([k_hi, k_lo, k_hi], axis=0))
         total -= local
         packed_x = [jnp.zeros((8, 128), f32)] * 2
         packed_y = [[jnp.zeros((8, 128), f32)] * 2 for _ in range(2)]
@@ -359,10 +389,10 @@
                     + jnp.where(seam_high, pltpu.roll(turned, 1, 0), 0.0)
                 )
                 both.append(block)
-            left, right = both
+            lower, upper = both
             both = [
-                left + jnp.where(at_i[1], lane_roll(right, 7), 0.0),
-                right + jnp.where(at_i[0], lane_roll(left, -7), 0.0),
+                lower + jnp.where(at_i[1], lane_roll(upper, 7), 0.0),
+                upper + jnp.where(at_i[0], lane_roll(lower, -7), 0.0),
             ]
             for s in range(2):
                 packed_x[s] = jnp.where(slot_i[m], lane_roll(both[s], m - 7 * s), packed_x[s])
@@ -476,12 +506,12 @@
             column += g2[d]
     else:
         column = lax.fori_loop(1, npy, lambda d, carry: carry + g2[d], g2[0])
-    first = TILE_DEV * (px * npy + py)
+    first_tile = TILE_DEV * (px * npy + py)
     pieces = [
-        jnp.sum(jnp.where(wide == first + q, column, 0.0), axis=1, keepdims=True)
+        jnp.sum(jnp.where(wide == first_tile + q, column, 0.0), axis=1, keepdims=True)
         for q in range(TILE_DEV)
     ]
-    grad_ref[...] = jnp.concatenate(pieces, axis=1)[:FREQS]
+    grad_ref[...] = jnp.concatenate(pieces, axis=1)[:FREQS].T
 
 
 def on_device(npx, npy, adjoint, zone_ids, resist, tile_map, materials):
@@ -489,17 +519,27 @@
     view = adjoint.reshape(2, 8, 8, 128).transpose(0, 2, 1, 3).reshape(128, 128)
     width = -(-TILE_DEV * npx * npy // 128) * 128
     vmem = pl.BlockSpec(memory_space=pltpu.VMEM)
-    smem = pl.BlockSpec(memory_space=pltpu.SMEM)
+    hbm = pl.BlockSpec(memory_space=pltpu.HBM)
+    smem = pltpu.SMEM
     dma = pltpu.SemaphoreType.DMA
     out, grad = pl.pallas_call(
         functools.partial(body, npx, npy),
         out_shape=(
             jax.ShapeDtypeStruct((FREQS * 128, 128), f32),
-            jax.ShapeDtypeStruct((FREQS, TILE_DEV), f32),
+            jax.ShapeDtypeStruct((TILE_DEV, FREQS), f32),
         ),
-        in_specs=[vmem] + [smem] * 4 + [vmem] * 5,
+        in_specs=[hbm] * 8,
         out_specs=(vmem, vmem),
         scratch_shapes=[
+            pltpu.VMEM((128, 128), f32),
+            smem(zone_ids.shape, jnp.int32),
+            smem(resist.shape, f32),
+            smem(tile_map.shape, jnp.int32),
+            smem(materials.shape, f32),
+            pltpu.VMEM((1152, 128), jnp.bfloat16),
+            pltpu.VMEM((1152, 128), jnp.bfloat16),
+            pltpu.VMEM((16, 128), f32),
+            dma((8,)),
             pltpu.VMEM((FREQS, 16, 8, 128), f32),
             pltpu.VMEM((2, FREQS, 8, 128), f32),
             pltpu.VMEM((2, 2, FREQS, 8, 128), f32),
@@ -520,11 +560,11 @@
             dma((npy,)),
         ],
         compiler_params=pltpu.CompilerParams(
-            collective_id=0, has_side_effects=True, vmem_limit_bytes=32 * 1024 * 1024
+            collective_id=0, has_side_effects=True, vmem_limit_bytes=63 * 1024 * 1024
         ),
     )(view, zone_ids, resist, tile_map, materials, *[jnp.asarray(item) for item in tables()])
     applied = out.reshape(FREQS, 2, 8, 8, 128).transpose(0, 1, 3, 2, 4)
-    return (applied.reshape(FREQS, 2, 1, CHANNELS, 1024), grad)
+    return (applied.reshape(FREQS, 2, 1, CHANNELS, 1024), grad.T)
 
 
 def solution(mesh):

time: 22.4 us -> 16.3 us (0.73); the launches traced: 22 us -> 16.2 us
  local copies, waits for them, and re-layouts: 8.55 us -> 2.18 us
  Pallas kernels: 12.7 us -> 13.3 us
    unnamed x22 -> x4, local copies, waits for them, and re-layouts: 8.55 us -> 2.18 us
    pallas_call x1, Pallas kernels: 12.7 us -> 13.3 us  [on_device(): pl.pallas_call(functools.partial(body, npx, npy), out_shape=(jax.ShapeDty...]
where the time goes in v1:
time: 16.3 us; the launch traced here: 16.2 us
  Pallas kernels  13.3 us (82%)
  local copies, waits for them, and re-layouts  2.18 us (13%)
  between operations  0.65 us (4%)
    pallas_call x1, Pallas kernels, on_device(): pl.pallas_call(functools.partial(body, npx, npy), out_shape=(jax.ShapeDty...  13.3 us
    unnamed x4, local copies, waits for them, and re-layouts  2.18 us

profile of v1, /device:TPU:0, one launch (start us, length us, event | category | flops | bytes accessed | tf_op | source)
XLA Modules:
  0.0 16.2 jit_solution(18070262817691985183)
XLA Ops:
  0.6 13.3 %shard_map.95 = (f32[384,128]{1,0:T(8,128)}, f32[2,3]{1,0:T(2,128)}) custom-call(f32[128,128]{1,0:T(8,128)} %bitcast.12, s32[2,1,2]{2,1,0:T(1,128)} %zone_hbm.1, f32[2,1,2]{2,1,0:T(1,128)} %resist_hbm.1, s32[2,1,2]{2,1,0:T(1,128)} %tile_hbm.1, f32[3,8,14]{2,1,0:T(8,128)} %mat_hbm.1, bf16[1152,128]{1,0:T(8,128)(2,1)} %constant.6.clone.forward_hbm, ...), custom_call_target="tpu_custom_call" | custom-call | tf_op jit(solution)/shard_map/pallas_call | solution.py:525
  14.0 0.0 copy-start
  14.0 1.6 %copy.12 = f32[3,2,1,8,1024]{4,3,2,1,0:T(8,128)} copy(f32[3,2,1,8,1024]{4,3,2,1,0:T(8,128)} %bitcast.11) | data formatting | bytes 393216
  15.6 0.0 copy-done
  15.6 0.6 %copy.13 = f32[3,2]{0,1:T(2,128)} copy(f32[3,2]{0,1:T(2,128)S(1)} %bitcast.13) | data formatting | bytes 48
Async XLA Ops:
  14.0 1.6 %copy-start = (f32[2,3]{1,0:T(2,128)S(1)}, f32[2,3]{1,0:T(2,128)}, u32[]{:S(2)}) copy-start(f32[2,3]{1,0:T(2,128)} %get-tuple-element.5) | copy-start | bytes 76

commit v2 on v1

--- a/solution.py
+++ b/solution.py
@@ -123,18 +123,16 @@
     rx,
     ry,
     rc,
-    g1,
-    g2,
+    shares,
+    parts,
     x_send,
     x_recv,
     y_send,
     y_recv,
     c_send,
     c_recv,
-    g1_send,
-    g1_recv,
-    g2_send,
-    g2_recv,
+    g_send,
+    g_recv,
 ):
     f32 = jnp.float32
     loads = [
@@ -164,14 +162,15 @@
     def has_corner(i, j):
         return jnp.logical_and(has_x[i], has_y[j])
 
-    def peer_px(d):
-        return (lax.rem(px + d, npx), py)
-
-    def peer_py(d):
-        return (px, lax.rem(py + d, npy))
-
-    def over(count, step):
-        if count <= 8:
+    count = npx * npy
+    me = px * npy + py
+
+    def peer(d):
+        other = lax.rem(me + d, count)
+        return (other // npy, lax.rem(other, npy))
+
+    def each_peer(step):
+        if count <= 32:
             for d in range(1, count):
                 step(d)
         else:
@@ -182,16 +181,7 @@
     def greet(device):
         pl.semaphore_signal(barrier, inc=1, device_id=device, device_id_type=MESH)
 
-    over(npx, lambda d: greet(peer_px(d)))
-    over(npy, lambda d: greet(peer_py(d)))
-    for i, j in corners:
-
-        @pl.when(has_corner(i, j))
-        def _(i=i, j=j):
-            greet((to_x[i], to_y[j]))
-
-    x_sides = jnp.where(has_x[0], 1, 0) + jnp.where(has_x[1], 1, 0)
-    y_sides = jnp.where(has_y[0], 1, 0) + jnp.where(has_y[1], 1, 0)
+    each_peer(lambda d: greet(peer(d)))
 
     row = lax.broadcasted_iota(jnp.int32, (8, 128), 0)
     lane = lax.broadcasted_iota(jnp.int32, (8, 128), 1)
@@ -298,46 +288,41 @@
         energy_real += g[d][3][0] * real - g[d][3][1] * imag
         energy_imag += g[d][3][0] * imag
     energy_imag = 2.0 * energy_imag
-    width = g1.shape[2]
-    wide = lax.broadcasted_iota(jnp.int32, (8, width), 1)
-    wide_row = lax.broadcasted_iota(jnp.int32, (8, width), 0)
-    message = jnp.zeros((8, width), f32)
-    for f in range(FREQS):
-        density = GRAD_SCALE * (slopes[f][0] * energy_real + slopes[f][1] * energy_imag)
-        gathered = jnp.zeros((8, width), f32)
-        for a in range(2):
-            part = density[8 * a : 8 * a + 8]
-            for c in range(2):
-                mine = jnp.where(low, part, 0.0) if c == 0 else jnp.where(low, 0.0, part)
-                mine = jnp.sum(mine, axis=1, keepdims=True)
-                gathered += jnp.where(wide == tile_ref[a, 0, c], mine, 0.0)
-        gathered = jnp.sum(gathered, axis=0, keepdims=True)
-        message = jnp.where(wide_row == f, gathered, message)
-    g1[0] = message
-
-    pl.semaphore_wait(barrier, npx - 1 + npy - 1 + x_sides * y_sides)
-
-    def copy_g1(d):
-        return pltpu.make_async_remote_copy(
-            src_ref=g1.at[0],
-            dst_ref=g1.at[d],
-            send_sem=g1_send.at[d],
-            recv_sem=g1_recv.at[d],
-            device_id=peer_px(d),
+    owner = lax.broadcasted_iota(jnp.int32, (count, 128), 0)
+    place = lax.broadcasted_iota(jnp.int32, (count, 128), 1)
+    tile_at = jnp.where(place < TILE_DEV * FREQS, TILE_DEV * owner + place // FREQS, -1)
+    freq_at = lax.broadcasted_iota(jnp.int32, (1, 128), 1) % FREQS
+    densities = [
+        GRAD_SCALE * (slopes[f][0] * energy_real + slopes[f][1] * energy_imag)
+        for f in range(FREQS)
+    ]
+    table = jnp.zeros((count, 128), f32)
+    for a in range(2):
+        sums = [
+            jnp.sum(item[8 * a : 8 * a + 8], axis=0, keepdims=True) for item in densities
+        ]
+        for c in range(2):
+            entry = jnp.zeros((1, 128), f32)
+            for f in range(FREQS):
+                half = jnp.where(low[:1] == (c == 0), sums[f], 0.0)
+                entry = jnp.where(freq_at == f, jnp.sum(half, axis=1, keepdims=True), entry)
+            table += jnp.where(tile_at == tile_ref[a, 0, c], entry, 0.0)
+    shares[...] = table
+
+    pl.semaphore_wait(barrier, count - 1)
+
+    def send_share(d):
+        device = peer(d)
+        pltpu.make_async_remote_copy(
+            src_ref=shares.at[pl.ds(lax.rem(me + d, count), 1)],
+            dst_ref=parts.at[pl.ds(d, 1)],
+            send_sem=g_send.at[0],
+            recv_sem=g_recv.at[0],
+            device_id=device,
             device_id_type=MESH,
-        )
-
-    def copy_g2(d):
-        return pltpu.make_async_remote_copy(
-            src_ref=g2.at[0],
-            dst_ref=g2.at[d],
-            send_sem=g2_send.at[d],
-            recv_sem=g2_recv.at[d],
-            device_id=peer_py(d),
-            device_id_type=MESH,
-        )
-
-    over(npx, lambda d: copy_g1(d).start())
+        ).start()
+
+    each_peer(send_share)
 
     div = plus(plus(g[0][0], g[1][1]), g[2][2])
     sym = {}
@@ -455,13 +440,6 @@
         def _(s=s):
             copy_x(s, 1 - s).start()
 
-    over(npx, lambda d: copy_g1(d).wait())
-    column = g1[0]
-    for d in range(1, npx):
-        column += g1[d]
-    g2[0] = column
-    over(npy, lambda d: copy_g2(d).start())
-
     for s in range(2):
 
         @pl.when(has_x[s])
@@ -499,25 +477,19 @@
                     )
                 out_ref[pl.ds(128 * f + 64 * a + m, 8, stride=8), :] = block
 
-    over(npy, lambda d: copy_g2(d).wait())
-    if npy <= 8:
-        column = g2[0]
-        for d in range(1, npy):
-            column += g2[d]
-    else:
-        column = lax.fori_loop(1, npy, lambda d, carry: carry + g2[d], g2[0])
-    first_tile = TILE_DEV * (px * npy + py)
-    pieces = [
-        jnp.sum(jnp.where(wide == first_tile + q, column, 0.0), axis=1, keepdims=True)
-        for q in range(TILE_DEV)
-    ]
-    grad_ref[...] = jnp.concatenate(pieces, axis=1)[:FREQS].T
+    others = pl.ds(1, count - 1)
+    pltpu.make_async_copy(shares.at[others], parts.at[others], g_send.at[0]).wait()
+    pltpu.make_async_copy(shares.at[others], parts.at[others], g_recv.at[0]).wait()
+    parts[0:1] = shares[pl.ds(me, 1)]
+    total = jnp.sum(parts[...], axis=0, keepdims=True)
+    grad_ref[...] = jnp.concatenate(
+        [total[:, FREQS * q : FREQS * q + FREQS] for q in range(TILE_DEV)], axis=0
+    )
 
 
 def on_device(npx, npy, adjoint, zone_ids, resist, tile_map, materials):
     f32 = jnp.float32
     view = adjoint.reshape(2, 8, 8, 128).transpose(0, 2, 1, 3).reshape(128, 128)
-    width = -(-TILE_DEV * npx * npy // 128) * 128
     vmem = pl.BlockSpec(memory_space=pltpu.VMEM)
     hbm = pl.BlockSpec(memory_space=pltpu.HBM)
     smem = pltpu.SMEM
@@ -546,18 +518,16 @@
             pltpu.VMEM((2, FREQS, 8, 128), f32),
             pltpu.VMEM((2, 2, FREQS, 8, 128), f32),
             pltpu.VMEM((4, FREQS, 8, 128), f32),
-            pltpu.VMEM((npx, 8, width), f32),
-            pltpu.VMEM((npy, 8, width), f32),
+            pltpu.VMEM((npx * npy, 128), f32),
+            pltpu.VMEM((npx * npy, 128), f32),
             dma((2,)),
             dma((2,)),
             dma((2,)),
             dma((2,)),
             dma((4,)),
             dma((4,)),
-            dma((npx,)),
-            dma((npx,)),
-            dma((npy,)),
-            dma((npy,)),
+            dma((1,)),
+            dma((1,)),
         ],
         compiler_params=pltpu.CompilerParams(
             collective_id=0, has_side_effects=True, vmem_limit_bytes=63 * 1024 * 1024

time: 16.3 us -> 14.7 us (0.902)
  Pallas kernels: 13.3 us -> 11.7 us
    pallas_call x1, Pallas kernels: 13.3 us -> 11.7 us  [on_device(): pl.pallas_call(functools.partial(body, npx, npy), out_shape=(jax.ShapeDty...]
where the time goes in v2:
time: 14.7 us; the launch traced here: 14.5 us
  Pallas kernels  11.7 us (80%)
  local copies, waits for them, and re-layouts  2.18 us (15%)
  between operations  0.65 us (4%)
    pallas_call x1, Pallas kernels, on_device(): pl.pallas_call(functools.partial(body, npx, npy), out_shape=(jax.ShapeDty...  11.7 us
    unnamed x4, local copies, waits for them, and re-layouts  2.18 us

profile of v2, /device:TPU:0, one launch (start us, length us, event | category | flops | bytes accessed | tf_op | source)
XLA Modules:
  0.0 14.5 jit_solution(579847770710873891)
XLA Ops:
  0.6 11.7 %shard_map.95 = (f32[384,128]{1,0:T(8,128)}, f32[2,3]{1,0:T(2,128)}) custom-call(f32[128,128]{1,0:T(8,128)} %bitcast.12, s32[2,1,2]{2,1,0:T(1,128)} %zone_hbm.1, f32[2,1,2]{2,1,0:T(1,128)} %resist_hbm.1, s32[2,1,2]{2,1,0:T(1,128)} %tile_hbm.1, f32[3,8,14]{2,1,0:T(8,128)} %mat_hbm.1, bf16[1152,128]{1,0:T(8,128)(2,1)} %constant.6.clone.forward_hbm, ...), custom_call_target="tpu_custom_call" | custom-call | tf_op jit(solution)/shard_map/pallas_call | solution.py:497
  12.3 0.0 copy-start
  12.3 1.6 %copy.12 = f32[3,2,1,8,1024]{4,3,2,1,0:T(8,128)} copy(f32[3,2,1,8,1024]{4,3,2,1,0:T(8,128)} %bitcast.11) | data formatting | bytes 393216
  14.0 0.0 copy-done
  14.0 0.6 %copy.13 = f32[3,2]{0,1:T(2,128)} copy(f32[3,2]{0,1:T(2,128)S(1)} %bitcast.13) | data formatting | bytes 48
Async XLA Ops:
  12.3 1.6 %copy-start = (f32[2,3]{1,0:T(2,128)S(1)}, f32[2,3]{1,0:T(2,128)}, u32[]{:S(2)}) copy-start(f32[2,3]{1,0:T(2,128)} %get-tuple-element.5) | copy-start | bytes 76

commit v3 on v2

--- a/solution.py
+++ b/solution.py
@@ -106,7 +106,7 @@
     forward_hbm,
     backward_hbm,
     weight_hbm,
-    out_ref,
+    out_hbm,
     grad_ref,
     x_ref,
     zone_ref,
@@ -117,6 +117,8 @@
     backward_ref,
     weight_ref,
     load_sem,
+    out_ref,
+    store_sem,
     held,
     sxb,
     syb,
@@ -308,21 +310,6 @@
                 entry = jnp.where(freq_at == f, jnp.sum(half, axis=1, keepdims=True), entry)
             table += jnp.where(tile_at == tile_ref[a, 0, c], entry, 0.0)
     shares[...] = table
-
-    pl.semaphore_wait(barrier, count - 1)
-
-    def send_share(d):
-        device = peer(d)
-        pltpu.make_async_remote_copy(
-            src_ref=shares.at[pl.ds(lax.rem(me + d, count), 1)],
-            dst_ref=parts.at[pl.ds(d, 1)],
-            send_sem=g_send.at[0],
-            recv_sem=g_recv.at[0],
-            device_id=device,
-            device_id_type=MESH,
-        ).start()
-
-    each_peer(send_share)
 
     div = plus(plus(g[0][0], g[1][1]), g[2][2])
     sym = {}
@@ -392,6 +379,21 @@
             for a in range(2):
                 syb[s, a, f] = packed_y[s][a]
 
+    pl.semaphore_wait(barrier, count - 1)
+
+    def send_share(d):
+        device = peer(d)
+        pltpu.make_async_remote_copy(
+            src_ref=shares.at[pl.ds(lax.rem(me + d, count), 1)],
+            dst_ref=parts.at[pl.ds(d, 1)],
+            send_sem=g_send.at[0],
+            recv_sem=g_recv.at[0],
+            device_id=device,
+            device_id_type=MESH,
+        ).start()
+
+    each_peer(send_share)
+
     def copy_x(s, there):
         return pltpu.make_async_remote_copy(
             src_ref=sxb.at[s],
@@ -458,6 +460,7 @@
         def _(i=i, j=j):
             copy_c(i, j, 2 * i + j).wait()
 
+    stores = []
     for f in range(FREQS):
         from_x = [rx[s, f] for s in range(2)]
         from_y = []
@@ -476,6 +479,12 @@
                         at_j[s], lane_roll(from_y[s][a], 8 * (7 * s - m)), 0.0
                     )
                 out_ref[pl.ds(128 * f + 64 * a + m, 8, stride=8), :] = block
+        stores.append(
+            pltpu.make_async_copy(
+                out_ref.at[pl.ds(128 * f, 128)], out_hbm.at[pl.ds(128 * f, 128)], store_sem.at[f]
+            )
+        )
+        stores[f].start()
 
     others = pl.ds(1, count - 1)
     pltpu.make_async_copy(shares.at[others], parts.at[others], g_send.at[0]).wait()
@@ -485,6 +494,30 @@
     grad_ref[...] = jnp.concatenate(
         [total[:, FREQS * q : FREQS * q + FREQS] for q in range(TILE_DEV)], axis=0
     )
+    for store in stores:
+        store.wait()
+
+
+def hand_on(out_from, grad_from, out_to, grad_to, out_held, grad_held, in_sem, out_sem):
+    chunks = in_sem.shape[0] - 1
+    rows = out_from.shape[0] // chunks
+    spans = [pl.ds(n * rows, rows) for n in range(chunks)]
+    routes = [(grad_from, grad_held, grad_to)] + [
+        (out_from.at[span], out_held.at[span], out_to.at[span]) for span in spans
+    ]
+    fetches = [
+        pltpu.make_async_copy(route[0], route[1], in_sem.at[n]) for n, route in enumerate(routes)
+    ]
+    stores = [
+        pltpu.make_async_copy(route[1], route[2], out_sem.at[n]) for n, route in enumerate(routes)
+    ]
+    for fetch in fetches:
+        fetch.start()
+    for fetch, store in zip(fetches, stores):
+        fetch.wait()
+        store.start()
+    for store in stores:
+        store.wait()
 
 
 def on_device(npx, npy, adjoint, zone_ids, resist, tile_map, materials):
@@ -501,7 +534,7 @@
             jax.ShapeDtypeStruct((TILE_DEV, FREQS), f32),
         ),
         in_specs=[hbm] * 8,
-        out_specs=(vmem, vmem),
+        out_specs=(hbm, vmem),
         scratch_shapes=[
             pltpu.VMEM((128, 128), f32),
             smem(zone_ids.shape, jnp.int32),
@@ -512,6 +545,8 @@
             pltpu.VMEM((1152, 128), jnp.bfloat16),
             pltpu.VMEM((16, 128), f32),
             dma((8,)),
+            pltpu.VMEM((FREQS * 128, 128), f32),
+            dma((FREQS,)),
             pltpu.VMEM((FREQS, 16, 8, 128), f32),
             pltpu.VMEM((2, FREQS, 8, 128), f32),
             pltpu.VMEM((2, 2, FREQS, 8, 128), f32),
@@ -533,6 +568,23 @@
             collective_id=0, has_side_effects=True, vmem_limit_bytes=63 * 1024 * 1024
         ),
     )(view, zone_ids, resist, tile_map, materials, *[jnp.asarray(item) for item in tables()])
+    chunks = 3
+    out, grad = pl.pallas_call(
+        hand_on,
+        out_shape=(
+            jax.ShapeDtypeStruct(out.shape, f32),
+            jax.ShapeDtypeStruct(grad.shape, f32),
+        ),
+        in_specs=[hbm] * 2,
+        out_specs=(hbm, hbm),
+        scratch_shapes=[
+            pltpu.VMEM(out.shape, f32),
+            pltpu.VMEM(grad.shape, f32),
+            dma((chunks + 1,)),
+            dma((chunks + 1,)),
+        ],
+        compiler_params=pltpu.CompilerParams(vmem_limit_bytes=63 * 1024 * 1024),
+    )(out, grad)
     applied = out.reshape(FREQS, 2, 8, 8, 128).transpose(0, 1, 3, 2, 4)
     return (applied.reshape(FREQS, 2, 1, CHANNELS, 1024), grad.T)
 

time: 14.7 us -> 14.1 us (0.959)
  local copies, waits for them, and re-layouts: 2.18 us -> 0 us
  Pallas kernels: 11.7 us -> 13.2 us
    unnamed x4 -> x0, local copies, waits for them, and re-layouts: 2.18 us -> none
    pallas_call x0 -> x1, Pallas kernels: none -> 1.61 us  [on_device(): pl.pallas_call(hand_on, out_shape=(jax.ShapeDtypeStruct(out.shape, f32),...]
where the time goes in v3:
time: 14.1 us; the launch traced here: 13.9 us
  Pallas kernels  13.2 us (94%)
  between operations  0.64 us (5%)
    pallas_call x1, Pallas kernels, on_device(): pl.pallas_call(functools.partial(body, npx, npy), out_shape=(jax.ShapeDty...  11.6 us
    pallas_call x1, Pallas kernels, on_device(): pl.pallas_call(hand_on, out_shape=(jax.ShapeDtypeStruct(out.shape, f32),...  1.61 us

profile of v3, /device:TPU:0, one launch (start us, length us, event | category | flops | bytes accessed | tf_op | source)
XLA Modules:
  0.0 13.9 jit_solution(645109506895153986)
XLA Ops:
  0.6 11.6 %shard_map.95 = (f32[384,128]{1,0:T(8,128)}, f32[2,3]{1,0:T(2,128)}) custom-call(f32[128,128]{1,0:T(8,128)} %bitcast.11, s32[2,1,2]{2,1,0:T(1,128)} %zone_hbm.1, f32[2,1,2]{2,1,0:T(1,128)} %resist_hbm.1, s32[2,1,2]{2,1,0:T(1,128)} %tile_hbm.1, f32[3,8,14]{2,1,0:T(8,128)} %mat_hbm.1, bf16[1152,128]{1,0:T(8,128)(2,1)} %constant.6.clone.forward_hbm, ...), custom_call_target="tpu_custom_call" | custom-call | tf_op jit(solution)/shard_map/pallas_call | solution.py:530
  12.3 1.6 %shard_map.96 = (f32[384,128]{1,0:T(8,128)}, f32[2,3]{1,0:T(2,128)}) custom-call(f32[384,128]{1,0:T(8,128)} %get-tuple-element.6.out_from, f32[2,3]{1,0:T(2,128)} %get-tuple-element.7.grad_from), custom_call_target="tpu_custom_call" | custom-call | tf_op jit(solution)/shard_map/pallas_call | solution.py:572
